TPU v7x, 32 devices: a whole 2x2x4 slice. The times are simulated.
32 devices in a mesh: dp: 16 (over z, y, x), mp: 2 (over core).
Axes of the slice: x: 2, y: 2, z: 4, core: 2. Of those that a mesh axis runs over, the one named last changes fastest.
Arguments:
- series_input: bfloat16 [23040, 1024], P('dp'), may hold values from -48 to 48
- lookback: int32 [1536], P('dp'), may hold values from 2 to 15, as said below
- slot_mask: int32 [1536, 15], P('dp'), may hold values 0 or 1
- offset: int32 [], replicated, may hold values from 1 to 14
- query_weight: bfloat16 [1024, 1024], P('dp', 'mp'), may hold values from -0.1875 to 0.1875
- key_weight: bfloat16 [1024, 1024], P('dp', 'mp'), may hold values from -0.1875 to 0.1875
- value_weight: bfloat16 [1024, 1024], P('dp', 'mp'), may hold values from -0.1875 to 0.1875
- out_weight: bfloat16 [1024, 1024], P('mp', 'dp'), may hold values from -0.375 to 0.375
- up_weight: bfloat16 [1024, 2048], P('dp', 'mp'), may hold values from -0.1875 to 0.1875
- down_weight: bfloat16 [2048, 1024], P('mp', 'dp'), may hold values from -0.1875 to 0.1875
- first_gain: bfloat16 [1024], P('dp'), may hold values from 0.25 to 1.75
- first_bias: bfloat16 [1024], P('dp'), may hold values from -3 to 3
- second_gain: bfloat16 [1024], P('dp'), may hold values from 0.25 to 1.75
- second_bias: bfloat16 [1024], P('dp'), may hold values from -3 to 3
- cotangent: bfloat16 [23040, 1024], P('dp'), may hold values from -24 to 24
Outputs:
- output: bfloat16 [23040, 1024], P(('dp', 'mp'))
- input_grad: float32 [23040, 1024], P('dp')
- query_grad: float32 [1024, 1024], P('dp', 'mp')
- key_grad: float32 [1024, 1024], P('dp', 'mp')
- value_grad: float32 [1024, 1024], P('dp', 'mp')
- out_grad: float32 [1024, 1024], P('mp', 'dp')
- up_grad: float32 [1024, 2048], P('dp', 'mp')
- down_grad: float32 [2048, 1024], P('mp', 'dp')
- first_gain_grad: float32 [1024], P('dp')
- first_bias_grad: float32 [1024], P('dp')
- second_gain_grad: float32 [1024], P('dp')
- second_bias_grad: float32 [1024], P('dp')
Inputs may be any that keep to these rules, and one draw needn't show every extreme that they name: The last series of each aligned block of 96 series has lookback 15.
All inputs are finite; a program needn't handle non-finite values. No bound on the sum of `slot_mask` on one device may be relied on, other than what follows from the above.
Results may differ from a plain program's by a relative error of at most 0.007.
The roundings to bfloat16 on the way count: a program that leaves them out, or rounds other values in their place, can miss the bound.
Values may be sent and summed in bfloat16 or wider, within the bound.
A program may use at most 192 MiB of HBM per device.

v0:
```python
import jax
import jax.numpy as jnp
from jax import lax
from jax.sharding import PartitionSpec as P

HDIM = 128
QBLOCK = 720


EPSILON = 1e-05
MASKED = -1e30
EXACT = lax.Precision.HIGHEST


def extended(block, sides, width):
    for axis, dim in sides:
        count = lax.axis_size(axis)
        forward = [(i, i + 1) for i in range(count - 1)]
        forward.append((count - 1, 0))
        backward = [(target, source) for source, target in forward]
        low = lax.ppermute(
            lax.slice_in_dim(block, block.shape[dim] - width, None, axis=dim), axis, forward
        )
        high = lax.ppermute(lax.slice_in_dim(block, 0, width, axis=dim), axis, backward)
        block = jnp.concatenate([low, block, high], axis=dim)
    return block


def erf_gelu(value):
    return 0.5 * value * (1.0 + lax.erf(value * 0.7071067811865476))


def layer_norm(value, gain, shift):
    centre = jnp.mean(value, axis=-1, keepdims=True)
    centred = value - centre
    spread = jnp.mean(centred * centred, axis=-1, keepdims=True)
    return centred * lax.rsqrt(spread + EPSILON) * gain + shift


def series_norm(wide, member, live_float, count):
    centre = jnp.dot(member, live_float * jnp.sum(wide, axis=1), precision=EXACT) / count
    centred = wide - jnp.dot(centre, member, precision=EXACT)[:, None]
    spread = (
        jnp.dot(member, live_float * jnp.sum(centred * centred, axis=1), precision=EXACT) / count
    )
    return centred * jnp.dot(lax.rsqrt(spread + EPSILON), member, precision=EXACT)[:, None]


def per_device(
    series_input,
    lookback,
    slot_mask,
    offset,
    query_weight,
    key_weight,
    value_weight,
    out_weight,
    up_weight,
    down_weight,
    first_gain,
    first_bias,
    second_gain,
    second_bias,
    cotangent,
):
    rows = series_input.shape[0]
    width = series_input.shape[1]
    slots = slot_mask.shape[1]
    reach = slots - 1
    span = rows + 2 * reach
    keyed = rows + reach
    scale = HDIM ** (-0.5)
    half = rows // lax.axis_size("mp")
    own_start = lax.axis_index("mp") * half
    slot_ids = lax.broadcasted_iota(jnp.int32, slot_mask.shape, 1)
    live_table = (
        (slot_ids >= slots - lookback[:, None]) & ((slot_mask > 0) | (slot_ids == slots - 1))
    ).astype(jnp.int32)
    live_wide = extended(live_table, (("dp", 0),), 2)
    series_count = jnp.sum(live_wide, axis=1).astype(jnp.float32) * width
    first = 2 * slots - reach - offset
    position = jnp.arange(span, dtype=jnp.int32) + first
    live_rows = lax.dynamic_slice_in_dim(live_wide.reshape(-1), first, span)
    live_float = live_rows.astype(jnp.float32)
    series_rows = position // slots
    member = (
        jnp.arange(live_wide.shape[0], dtype=jnp.int32)[:, None] == series_rows[None, :]
    ).astype(jnp.float32)
    wide = extended(series_input, (("dp", 0),), reach).astype(jnp.float32)
    gathered = (
        lax.all_gather(query_weight, "dp", axis=0, tiled=True),
        lax.all_gather(key_weight, "dp", axis=0, tiled=True),
        lax.all_gather(value_weight, "dp", axis=0, tiled=True),
        lax.all_gather(out_weight, "dp", axis=1, tiled=True),
        lax.all_gather(up_weight, "dp", axis=0, tiled=True),
        lax.all_gather(down_weight, "dp", axis=1, tiled=True),
        lax.all_gather(first_gain, "dp", axis=0, tiled=True),
        lax.all_gather(first_bias, "dp", axis=0, tiled=True),
        lax.all_gather(second_gain, "dp", axis=0, tiled=True),
        lax.all_gather(second_bias, "dp", axis=0, tiled=True),
    )
    (
        query_all,
        key_all,
        value_all,
        out_all,
        up_all,
        down_all,
        gain_one,
        bias_one,
        gain_two,
        bias_two,
    ) = gathered

    def front(value, gain, shift):
        normed_rows = series_norm(value, member, live_float, series_count)
        return (layer_norm(normed_rows, gain, shift), normed_rows)

    (act_first, normed), front_back = jax.vjp(
        front, wide, gain_one.astype(jnp.float32), bias_one.astype(jnp.float32)
    )
    act_low = act_first[:keyed].astype(jnp.bfloat16)
    local_heads = query_all.shape[1] // HDIM
    query = (
        jnp.dot(act_low, query_all, preferred_element_type=jnp.float32)
        .astype(jnp.bfloat16)
        .reshape(keyed, local_heads, HDIM)
    )
    keys = (
        jnp.dot(act_low, key_all, preferred_element_type=jnp.float32)
        .astype(jnp.bfloat16)
        .reshape(keyed, local_heads, HDIM)
    )
    values = (
        jnp.dot(act_low, value_all, preferred_element_type=jnp.float32)
        .astype(jnp.bfloat16)
        .reshape(keyed, local_heads, HDIM)
    )
    order = jnp.arange(keyed, dtype=jnp.int32)

    def block_scores(start):
        query_rows = slice(start + reach, start + reach + QBLOCK)
        key_rows = slice(start, start + QBLOCK + reach)
        raw = (
            jnp.einsum(
                "qhc,khc->hqk",
                query[query_rows],
                keys[key_rows],
                preferred_element_type=jnp.float32,
            )
            * scale
        )
        query_pos = order[query_rows][:, None]
        key_pos = order[key_rows][None, :]
        same = series_rows[query_rows][:, None] == series_rows[key_rows][None, :]
        opened = (live_rows[key_rows] > 0)[None, :] | (query_pos == key_pos)
        allowed = same & (query_pos >= key_pos) & opened
        return jnp.where(allowed[None], raw, MASKED)

    mixed_parts = []
    total_parts = []
    for start in range(0, rows, QBLOCK):
        masked = block_scores(start)
        top = jnp.max(masked, axis=-1, keepdims=True)
        expo = jnp.exp(masked - top)
        summed = jnp.sum(expo, axis=-1, keepdims=True)
        probs_low = (expo / summed).astype(jnp.bfloat16)
        block_out = jnp.einsum(
            "hqk,khc->qhc",
            probs_low,
            values[start : start + QBLOCK + reach],
            preferred_element_type=jnp.float32,
        )
        mixed_parts.append(block_out.astype(jnp.bfloat16).reshape(QBLOCK, local_heads * HDIM))
        total_parts.append(top + jnp.log(summed))
    mixed = jnp.concatenate(mixed_parts, axis=0)
    attn_part = jnp.dot(mixed, out_all, preferred_element_type=jnp.float32)
    normed_own = normed[reach : reach + rows]
    gain_two_f = gain_two.astype(jnp.float32)
    bias_two_f = bias_two.astype(jnp.float32)
    hidden_one = normed_own + lax.psum(attn_part, "mp")
    act_second, second_back = jax.vjp(layer_norm, hidden_one, gain_two_f, bias_two_f)
    second_low = act_second.astype(jnp.bfloat16)
    gate = jnp.dot(second_low, up_all, preferred_element_type=jnp.float32)
    inner_full, gelu_back = jax.vjp(erf_gelu, gate)
    inner = inner_full.astype(jnp.bfloat16)
    ffn_part = jnp.dot(inner, down_all, preferred_element_type=jnp.float32)
    layer_out = hidden_one + lax.psum(ffn_part, "mp")
    result = lax.dynamic_slice_in_dim(layer_out, own_start, half).astype(jnp.bfloat16)
    grad_out = cotangent.astype(jnp.float32)
    grad_ffn = grad_out.astype(jnp.bfloat16)
    down_delta = jnp.einsum("tf,td->fd", inner, grad_ffn, preferred_element_type=jnp.float32)
    grad_inner = jnp.einsum("td,fd->tf", grad_ffn, down_all, preferred_element_type=jnp.float32)
    grad_gate = gelu_back(grad_inner)[0].astype(jnp.bfloat16)
    up_delta = jnp.einsum("td,tf->df", second_low, grad_gate, preferred_element_type=jnp.float32)
    second_part = jnp.einsum("tf,df->td", grad_gate, up_all, preferred_element_type=jnp.float32)
    grad_second = lax.psum(second_part, "mp")
    grad_hidden, gain_two_delta, bias_two_delta = second_back(grad_second)
    grad_hidden = grad_hidden + grad_out
    grad_attn = grad_hidden.astype(jnp.bfloat16)
    out_delta = jnp.einsum("tc,td->cd", mixed, grad_attn, preferred_element_type=jnp.float32)
    grad_mixed = jnp.einsum(
        "td,cd->tc", grad_attn, out_all, preferred_element_type=jnp.float32
    ).astype(jnp.bfloat16)
    grad_query = jnp.zeros((keyed, local_heads, HDIM), jnp.float32)
    grad_keys = jnp.zeros((keyed, local_heads, HDIM), jnp.float32)
    grad_values = jnp.zeros((keyed, local_heads, HDIM), jnp.float32)
    for number, start in enumerate(range(0, rows, QBLOCK)):
        probs = jnp.exp(block_scores(start) - total_parts[number])
        grad_block = grad_mixed[start : start + QBLOCK].reshape(QBLOCK, local_heads, HDIM)
        key_rows = slice(start, start + QBLOCK + reach)
        query_rows = slice(start + reach, start + reach + QBLOCK)
        grad_probs = jnp.einsum(
            "qhc,khc->hqk", grad_block, values[key_rows], preferred_element_type=jnp.float32
        )
        grad_values = grad_values.at[key_rows].add(
            jnp.einsum(
                "hqk,qhc->khc",
                probs.astype(jnp.bfloat16),
                grad_block,
                preferred_element_type=jnp.float32,
            )
        )
        inner_sum = jnp.sum(grad_probs * probs, axis=-1, keepdims=True)
        grad_scores = (probs * (grad_probs - inner_sum)).astype(jnp.bfloat16)
        grad_query = grad_query.at[query_rows].add(
            jnp.einsum(
                "hqk,khc->qhc", grad_scores, keys[key_rows], preferred_element_type=jnp.float32
            )
            * scale
        )
        grad_keys = grad_keys.at[key_rows].add(
            jnp.einsum(
                "hqk,qhc->khc", grad_scores, query[query_rows], preferred_element_type=jnp.float32
            )
            * scale
        )
    query_low = grad_query.reshape(keyed, local_heads * HDIM).astype(jnp.bfloat16)
    keys_low = grad_keys.reshape(keyed, local_heads * HDIM).astype(jnp.bfloat16)
    values_low = grad_values.reshape(keyed, local_heads * HDIM).astype(jnp.bfloat16)
    query_delta = jnp.einsum("td,tc->dc", act_low, query_low, preferred_element_type=jnp.float32)
    key_delta = jnp.einsum("td,tc->dc", act_low, keys_low, preferred_element_type=jnp.float32)
    value_delta = jnp.einsum("td,tc->dc", act_low, values_low, preferred_element_type=jnp.float32)
    grad_first = jnp.einsum("tc,dc->td", query_low, query_all, preferred_element_type=jnp.float32)
    grad_first = grad_first + jnp.einsum(
        "tc,dc->td", keys_low, key_all, preferred_element_type=jnp.float32
    )
    grad_first = grad_first + jnp.einsum(
        "tc,dc->td", values_low, value_all, preferred_element_type=jnp.float32
    )
    grad_first = lax.psum(grad_first, "mp")
    edge_zeros = jnp.zeros((reach, width), jnp.float32)
    full_first = jnp.concatenate([grad_first, edge_zeros], axis=0)
    full_normed = jnp.concatenate([edge_zeros, grad_hidden, edge_zeros], axis=0)
    grad_wide, gain_one_delta, bias_one_delta = front_back((full_first, full_normed))
    rims = jnp.concatenate([grad_wide[:reach], grad_wide[span - reach :]], axis=0)
    returned = extended(rims, (("dp", 0),), reach)
    grad_input = grad_wide[reach : reach + rows]
    grad_input = grad_input.at[:reach].add(returned[:reach])
    grad_input = grad_input.at[rows - reach :].add(returned[3 * reach :])
    sums = (
        lax.psum_scatter(query_delta, "dp", scatter_dimension=0, tiled=True),
        lax.psum_scatter(key_delta, "dp", scatter_dimension=0, tiled=True),
        lax.psum_scatter(value_delta, "dp", scatter_dimension=0, tiled=True),
        lax.psum_scatter(out_delta, "dp", scatter_dimension=1, tiled=True),
        lax.psum_scatter(up_delta, "dp", scatter_dimension=0, tiled=True),
        lax.psum_scatter(down_delta, "dp", scatter_dimension=1, tiled=True),
        lax.psum_scatter(gain_one_delta, "dp", scatter_dimension=0, tiled=True),
        lax.psum_scatter(bias_one_delta, "dp", scatter_dimension=0, tiled=True),
        lax.psum_scatter(gain_two_delta, "dp", scatter_dimension=0, tiled=True),
        lax.psum_scatter(bias_two_delta, "dp", scatter_dimension=0, tiled=True),
    )
    return (
        result,
        grad_input,
        sums[0],
        sums[1],
        sums[2],
        sums[3],
        sums[4],
        sums[5],
        sums[6],
        sums[7],
        sums[8],
        sums[9],
    )


def solution(mesh):
    return jax.shard_map(
        per_device,
        mesh=mesh,
        in_specs=(
            P("dp", None),
            P("dp"),
            P("dp", None),
            P(),
            P("dp", "mp"),
            P("dp", "mp"),
            P("dp", "mp"),
            P("mp", "dp"),
            P("dp", "mp"),
            P("mp", "dp"),
            P("dp"),
            P("dp"),
            P("dp"),
            P("dp"),
            P("dp", None),
        ),
        out_specs=(
            P(("dp", "mp"), None),
            P("dp", None),
            P("dp", "mp"),
            P("dp", "mp"),
            P("dp", "mp"),
            P("mp", "dp"),
            P("dp", "mp"),
            P("mp", "dp"),
            P("dp"),
            P("dp"),
            P("dp"),
            P("dp"),
        ),
        check_vma=False,
    )
```

profile of v0, /device:TPU:0, one launch (start us, length us, event | category | flops | bytes accessed | tf_op | source)
XLA Modules:
  0.0 1114.2 jit_solution(8607482222271177787)
XLA Ops:
  27.1 43.1 %all-reduce.14 = (bf16[1024]{0:T(1024)(128)(2,1)S(1)}, bf16[1024]{0:T(1024)(128)(2,1)S(1)}, bf16[1024]{0:T(1024)(128)(2,1)S(1)}, bf16[1024]{0:T(1024)(128)(2,1)S(1)}) all-reduce(bf16[1024]{0:T(1024)(128)(2,1)S(1)} %dynamic-update-slice.25, bf16[1024]{0:T(1024)(128)(2,1)S(1)} %dynamic-update-slice.24, ...), channel_id=1, replica_groups=mesh['dp'=16,'mp'=2] {'dp'}, use_global_device_ids=true, to_apply=%add.5 | all-reduce | flops 4096 | bytes 16384
  73.3 12.7 %concatenate.31 = bf16[1468,1024]{1,0:T(8,128)(2,1)S(1)} concatenate(bf16[14,1024]{1,0:T(8,128)(2,1)S(1)} %collective-permute-done, bf16[1440,1024]{1,0:T(8,128)(2,1)} %param.31, bf16[14,1024]{1,0:T(8,128)(2,1)S(1)} %collective-permute-done.1), dimensions={0} | concatenate | bytes 6012928 | tf_op jit(solution)/shard_map/concatenate | solution.py:25
  104.9 21.4 %all-gather.9.cloned.1.call-done = bf16[1024,512]{1,0:T(8,128)(2,1)} async-done(((bf16[64,512]{1,0:T(8,128)(2,1)}), bf16[1024,512]{1,0:T(8,128)(2,1)}) %all-gather.9.cloned.1.call-update) | async-done | bytes 1048592 | tf_op jit(solution)/shard_map/all_gather | solution.py:91
  131.4 51.8 %all-gather.7.cloned.1.call-done = bf16[1024,512]{1,0:T(8,128)(2,1)} async-done(((bf16[64,512]{1,0:T(8,128)(2,1)}), bf16[1024,512]{1,0:T(8,128)(2,1)}) %all-gather.7.cloned.1.call-update) | async-done | bytes 1048592 | tf_op jit(solution)/shard_map/all_gather | solution.py:93
  207.0 32.9 %all-gather.13.cloned.1.call-done = bf16[512,1024]{0,1:T(8,128)(2,1)} async-done(((bf16[512,64]{0,1:T(8,128)(2,1)}), bf16[512,1024]{0,1:T(8,128)(2,1)}) %all-gather.13.cloned.1.call-update) | async-done | bytes 1048592 | tf_op jit(solution)/shard_map/all_gather | solution.py:94
  239.9 6.0 fusion.97
  247.3 28.9 %all-reduce.19.cloned.1.call-done = f32[1440,1024]{1,0:T(8,128)} async-done(((f32[1440,1024]{1,0:T(8,128)}), f32[1440,1024]{1,0:T(8,128)}) %all-reduce.19.cloned.1.call-update) | async-done | bytes 5898256 | tf_op jit(solution)/shard_map/psum | solution.py:181
  276.1 5.3 fusion.85
  286.7 54.4 %all-gather.15.cloned.1.call-done = bf16[1024,1024]{1,0:T(8,128)(2,1)} async-done(((bf16[64,1024]{1,0:T(8,128)(2,1)}), bf16[1024,1024]{1,0:T(8,128)(2,1)}) %all-gather.15.cloned.1.call-update) | async-done | bytes 2097168 | tf_op jit(solution)/shard_map/all_gather | solution.py:95
  341.1 8.3 fusion.98
  349.3 54.3 %all-gather.17.cloned.1.call-done = bf16[1024,1024]{0,1:T(8,128)(2,1)} async-done(((bf16[1024,64]{0,1:T(8,128)(2,1)}), bf16[1024,1024]{0,1:T(8,128)(2,1)}) %all-gather.17.cloned.1.call-update) | async-done | bytes 2097168 | tf_op jit(solution)/shard_map/all_gather | solution.py:96
  403.6 9.8 add_convert_fusion
  415.0 5.2 fusion.100
  420.3 8.9 fusion.99
  429.3 21.1 %all-reduce.21.cloned.1.call-done = f32[1440,1024]{1,0:T(8,128)} async-done(((f32[1440,1024]{1,0:T(8,128)}), f32[1440,1024]{1,0:T(8,128)}) %all-reduce.21.cloned.1.call-update) | async-done | bytes 5898256 | tf_op jit(solution)/shard_map/psum | solution.py:197
  450.4 5.9 multiply_reduce_fusion.5
  456.4 4.5 fusion.84
  503.9 5.8 scatter-add.26
  531.5 8.4 fusion.106
  540.0 10.1 fusion.107
  550.2 6.8 fusion.26
  557.0 5.1 fusion.105
  562.4 5.3 fusion.103
  568.5 17.7 %concatenate.34 = f32[1468,1024]{1,0:T(8,128)} concatenate(f32[14,1024]{1,0:T(8,128)S(1)} %broadcast_in_dim.43, f32[1440,1024]{1,0:T(8,128)} %copy-done.8, f32[14,1024]{1,0:T(8,128)S(1)} %broadcast_in_dim.43), dimensions={0} | concatenate | bytes 12025856 | tf_op jit(solution)/shard_map/concatenate | solution.py:254
  586.2 5.7 fusion.104
  592.0 6.4 multiply_reduce_fusion.2
  618.9 77.8 %all-reduce.12 = (f32[1024]{0:T(1024)S(1)}, f32[1024]{0:T(1024)S(1)}, f32[1024]{0:T(1024)S(1)}, f32[1024]{0:T(1024)S(1)}) all-reduce(f32[1024]{0:T(1024)S(1)} %get-tuple-element.110, f32[1024]{0:T(1024)S(1)} %get-tuple-element.112, f32[1024]{0:T(1024)S(1)} %get-tuple-element.108, ...), channel_id=8, replica_groups=mesh['dp'=16,'mp'=2] {'dp'}, use_global_device_ids=true, to_apply=%region_30.31.clone | all-reduce | flops 4096 | bytes 32768
  707.2 75.6 %reduce-scatter.17.cloned.1.call-done = f32[1024,64]{0,1:T(8,128)} async-done(((f32[1024,1024]{0,1:T(8,128)}), f32[1024,64]{0,1:T(8,128)}) %reduce-scatter.17.cloned.1.call-update) | async-done | bytes 262160 | tf_op jit(solution)/shard_map/reduce_scatter | solution.py:267
  782.9 82.8 %reduce-scatter.13.cloned.1.call-done = f32[512,64]{0,1:T(8,128)} async-done(((f32[512,1024]{0,1:T(8,128)}), f32[512,64]{0,1:T(8,128)}) %reduce-scatter.13.cloned.1.call-update) | async-done | bytes 131088 | tf_op jit(solution)/shard_map/reduce_scatter | solution.py:265
  865.7 80.7 %reduce-scatter.11.cloned.1.call-done = f32[64,512]{1,0:T(8,128)} async-done(((f32[1024,512]{1,0:T(8,128)}), f32[64,512]{1,0:T(8,128)}) %reduce-scatter.11.cloned.1.call-update) | async-done | bytes 131088 | tf_op jit(solution)/shard_map/reduce_scatter | solution.py:264
  946.4 80.6 %reduce-scatter.7.cloned.1.call-done = f32[64,512]{1,0:T(8,128)} async-done(((f32[1024,512]{1,0:T(8,128)}), f32[64,512]{1,0:T(8,128)}) %reduce-scatter.7.cloned.1.call-update) | async-done | bytes 131088 | tf_op jit(solution)/shard_map/reduce_scatter | solution.py:262
  1027.0 80.5 %reduce-scatter.9.cloned.1.call-done = f32[64,512]{1,0:T(8,128)} async-done(((f32[1024,512]{1,0:T(8,128)}), f32[64,512]{1,0:T(8,128)}) %reduce-scatter.9.cloned.1.call-update) | async-done | bytes 131088 | tf_op jit(solution)/shard_map/reduce_scatter | solution.py:263
  (289 shorter events, 173.2 us)
Async XLA Ops:
  7.2 91.8 %all-gather.11.cloned.1.call-start = ((), (), s32[]{:S(2)}) async-start(), calls=%async_computation.8 | async-start | bytes 1114112 | tf_op jit(solution)/shard_map/all_gather | solution.py:92
  7.9 118.4 %all-gather.9.cloned.1.call-start = ((), (), s32[]{:S(2)}) async-start(), calls=%async_computation.7 | async-start | bytes 1114112 | tf_op jit(solution)/shard_map/all_gather | solution.py:91
  8.7 174.5 %all-gather.7.cloned.1.call-start = ((), (), s32[]{:S(2)}) async-start(), calls=%async_computation.6 | async-start | bytes 1114112 | tf_op jit(solution)/shard_map/all_gather | solution.py:93
  9.4 230.5 %all-gather.13.cloned.1.call-start = ((), (), s32[]{:S(2)}) async-start(), calls=%async_computation.9 | async-start | bytes 1114112 | tf_op jit(solution)/shard_map/all_gather | solution.py:94
  11.0 59.3 %collective-permute-start.2 = (s32[2,15]{0,1:T(8,128)S(1)}, s32[2,15]{0,1:T(8,128)S(1)}, u32[]{:S(2)}, u32[]{:S(2)}) collective-permute-start(s32[2,15]{0,1:T(8,128)S(1)} %get-tuple-element.156), channel_id=1, source_target_pairs={{0,2},{2,4},{4,6},{6,8},{8,10},{10,12},{12,14},{14,16},{16,18},{18... | collective-permute-start | bytes 368 | tf_op jit(solution)/shard_map/ppermute | solution.py:21
  13.9 56.4 %collective-permute-start.3 = (s32[2,15]{0,1:T(8,128)S(1)}, s32[2,15]{0,1:T(8,128)S(1)}, u32[]{:S(2)}, u32[]{:S(2)}) collective-permute-start(s32[2,15]{0,1:T(8,128)S(1)} %get-tuple-element.157), channel_id=1, source_target_pairs={{2,0},{4,2},{6,4},{8,6},{10,8},{12,10},{14,12},{16,14},{18,16},{20... | collective-permute-start | bytes 368 | tf_op jit(solution)/shard_map/ppermute | solution.py:24
  18.7 54.6 %collective-permute-start.1 = (bf16[14,1024]{1,0:T(8,128)(2,1)S(1)}, bf16[14,1024]{1,0:T(8,128)(2,1)S(1)}, u32[]{:S(2)}, u32[]{:S(2)}) collective-permute-start(bf16[14,1024]{1,0:T(8,128)(2,1)S(1)} %get-tuple-element.140), channel_id=1, source_target_pairs={{2,0},{4,2},{6,4},{8,6},{10,8},{12,10},{14,12},{16,14},{18,16},{20... | collective-permute-start | bytes 86024 | tf_op jit(solution)/shard_map/ppermute | solution.py:24
  20.8 52.6 %collective-permute-start = (bf16[14,1024]{1,0:T(8,128)(2,1)S(1)}, bf16[14,1024]{1,0:T(8,128)(2,1)S(1)}, u32[]{:S(2)}, u32[]{:S(2)}) collective-permute-start(bf16[14,1024]{1,0:T(8,128)(2,1)S(1)} %get-tuple-element.141), channel_id=1, source_target_pairs={{0,2},{2,4},{4,6},{6,8},{8,10},{10,12},{12,14},{14,16},{16,18},{18... | collective-permute-start | bytes 86024 | tf_op jit(solution)/shard_map/ppermute | solution.py:21
  20.8 255.3 %all-reduce.19.cloned.1.call-start = ((), (), s32[]{:S(2)}) async-start(), calls=%async_computation.10 | async-start | bytes 11796480 | tf_op jit(solution)/shard_map/psum | solution.py:181
  21.6 67.1 %copy-start.34 = (s32[1468]{0:T(1024)}, s32[1468]{0:T(1024)S(1)}, u32[]{:S(2)}) copy-start(s32[1468]{0:T(1024)S(1)} %add_select_fusion) | copy-start | bytes 17620
  70.2 27.7 %copy-start.36 = (f32[1024]{0:T(1024)}, f32[1024]{0:T(1024)S(1)}, u32[]{:S(2)}) copy-start(f32[1024]{0:T(1024)S(1)} %convert_element_type.109) | copy-start | bytes 12292
  70.4 18.0 %copy-start.38 = (s32[100]{0:T(128)}, s32[100]{0:T(128)S(1)}, u32[]{:S(2)}) copy-start(s32[100]{0:T(128)S(1)} %get-tuple-element.132) | copy-start | bytes 1204
  70.7 17.6 %copy-start.26 = (s32[1500]{0:T(1024)}, s32[1500]{0:T(1024)S(1)}, u32[]{:S(2)}) copy-start(s32[1500]{0:T(1024)S(1)} %reshape.571) | copy-start | bytes 18004
  86.0 9.3 copy-start
  103.8 95.6 %copy-start.10 = (bf16[734,4,128]{2,1,0:T(4,128)(2,1)}, bf16[734,4,128]{2,1,0:T(4,128)(2,1)S(1)}, u32[]{:S(2)}) copy-start(bf16[734,4,128]{2,1,0:T(4,128)(2,1)S(1)} %slice.327) | copy-start | bytes 2254852
  131.4 67.9 %copy-start.14 = (bf16[90,4,8,128]{3,2,1,0:T(8,128)(2,1)}, bf16[90,4,8,128]{3,2,1,0:T(8,128)(2,1)S(1)}, u32[]{:S(2)}) copy-start(bf16[90,4,8,128]{3,2,1,0:T(8,128)(2,1)S(1)} %get-tuple-element.144) | copy-start | bytes 2211844
  245.9 95.2 %all-gather.15.cloned.1.call-start = ((), (), s32[]{:S(2)}) async-start(), calls=%async_computation.11 | async-start | bytes 2228224 | tf_op jit(solution)/shard_map/all_gather | solution.py:95
  246.5 157.1 %all-gather.17.cloned.1.call-start = ((), (), s32[]{:S(2)}) async-start(), calls=%async_computation.12 | async-start | bytes 2228224 | tf_op jit(solution)/shard_map/all_gather | solution.py:96
  247.2 203.2 %all-reduce.21.cloned.1.call-start = ((), (), s32[]{:S(2)}) async-start(), calls=%async_computation.13 | async-start | bytes 11796480 | tf_op jit(solution)/shard_map/psum | solution.py:197
  403.6 11.4 %copy-start.40 = (bf16[1024,1024]{1,0:T(8,128)(2,1)S(1)}, bf16[1024,1024]{1,0:T(8,128)(2,1)}, u32[]{:S(2)}) copy-start(bf16[1024,1024]{1,0:T(8,128)(2,1)} %all-gather.15.cloned.1.call-done) | copy-start | bytes 6291460
  420.2 171.7 %all-reduce.23.cloned.1.call-start = ((), (), s32[]{:S(2)}) async-start(), calls=%async_computation.20 | async-start | bytes 23724032 | tf_op jit(solution)/shard_map/psum | solution.py:188
  501.5 10.6 copy-start.9
  531.2 176.0 %reduce-scatter.15.cloned.1.call-start = ((), (), s32[]{:S(2)}) async-start(), calls=%async_computation.18 | async-start | bytes 4456448 | tf_op jit(solution)/shard_map/reduce_scatter | solution.py:266
  539.9 242.9 %reduce-scatter.17.cloned.1.call-start = ((), (), s32[]{:S(2)}) async-start(), calls=%async_computation.19 | async-start | bytes 4456448 | tf_op jit(solution)/shard_map/reduce_scatter | solution.py:267
  550.1 315.6 %reduce-scatter.13.cloned.1.call-start = ((), (), s32[]{:S(2)}) async-start(), calls=%async_computation.17 | async-start | bytes 2228224 | tf_op jit(solution)/shard_map/reduce_scatter | solution.py:265
  557.0 389.4 %reduce-scatter.11.cloned.1.call-start = ((), (), s32[]{:S(2)}) async-start(), calls=%async_computation.16 | async-start | bytes 2228224 | tf_op jit(solution)/shard_map/reduce_scatter | solution.py:264
  562.2 464.8 %reduce-scatter.7.cloned.1.call-start = ((), (), s32[]{:S(2)}) async-start(), calls=%async_computation.14 | async-start | bytes 2228224 | tf_op jit(solution)/shard_map/reduce_scatter | solution.py:262
  567.7 539.7 %reduce-scatter.9.cloned.1.call-start = ((), (), s32[]{:S(2)}) async-start(), calls=%async_computation.15 | async-start | bytes 2228224 | tf_op jit(solution)/shard_map/reduce_scatter | solution.py:263
  592.0 10.3 slice-start.8
  602.4 9.7 slice-start
  610.2 88.8 %collective-permute-start.4 = (f32[14,1024]{1,0:T(8,128)S(1)}, f32[14,1024]{1,0:T(8,128)S(1)}, u32[]{:S(2)}, u32[]{:S(2)}) collective-permute-start(f32[14,1024]{1,0:T(8,128)S(1)} %get-tuple-element.135), channel_id=1, source_target_pairs={{0,2},{2,4},{4,6},{6,8},{8,10},{10,12},{12,14},{14,16},{16,18},{18... | collective-permute-start | bytes 172040 | tf_op jit(solution)/shard_map/ppermute | solution.py:21
  699.0 5.8 collective-permute-start.5
  (45 other events, 196.4 us)
Sparse Core Ops, SparseCore 0:
  10.8 58.3 all-gather.10
  71.9 54.3 all-gather.8
  129.0 54.0 all-gather.6
  185.8 54.0 all-gather.12
  246.0 30.0 all-reduce.18
  279.1 61.8 all-gather.14
  344.2 59.3 all-gather.16
  420.4 29.9 all-reduce.20
  531.4 49.3 all-reduce.22
  583.6 99.8 reduce-scatter.14
  686.5 96.2 reduce-scatter.16
  785.7 79.9 reduce-scatter.12
  868.6 77.6 reduce-scatter.10
  949.2 77.7 reduce-scatter.6
  1029.8 77.6 reduce-scatter.8
where the time goes:
time: 1120 us; the launch traced here: 1110 us
  waiting for transfers between devices  672 us (60%)
  matrix products  137 us (12%)
  blocking collectives  121 us (11%)
  local copies, waits for them, and re-layouts  83.4 us (7%)
  other arithmetic  71.6 us (6%)
  between operations  17.4 us (2%)
  starting transfers between devices  12 us (1%)
    unnamed x2, blocking collectives  121 us
    reduce_scatter x1, waiting for transfers between devices, per_device(): lax.psum_scatter(out_delta, 'dp', scatter_dimension=1, tiled=True)  82.8 us
    reduce_scatter x1, waiting for transfers between devices, per_device(): lax.psum_scatter(value_delta, 'dp', scatter_dimension=0, tiled=True)  80.7 us
    reduce_scatter x1, waiting for transfers between devices, per_device(): lax.psum_scatter(query_delta, 'dp', scatter_dimension=0, tiled=True)  80.6 us
    reduce_scatter x1, waiting for transfers between devices, per_device(): lax.psum_scatter(key_delta, 'dp', scatter_dimension=0, tiled=True)  80.5 us
    reduce_scatter x1, waiting for transfers between devices, per_device(): lax.psum_scatter(down_delta, 'dp', scatter_dimension=1, tiled=True)  75.6 us
    all_gather x1, waiting for transfers between devices, per_device(): lax.all_gather(up_weight, 'dp', axis=0, tiled=True)  54.4 us
    all_gather x1, waiting for transfers between devices, per_device(): lax.all_gather(down_weight, 'dp', axis=1, tiled=True)  54.3 us
  transfers between devices with their start and end apart: 21, of which 13 were waited for; matrix products, arithmetic and copies ran while one was open for 17% of the time, Pallas kernels for 0%

commit v1 on v0

v1 whole, which is shorter than its diff:
```python
import functools

import jax
import jax.numpy as jnp
from jax import lax
from jax.experimental import pallas as pl
from jax.experimental.pallas import tpu as pltpu
from jax.sharding import PartitionSpec as P

HDIM = 128
PAD = 16
EPSILON = 1e-05
MASKED = -1e30
MESH = pl.DeviceIdType.MESH
LANES = 128
JOB = 512
BF16 = jnp.bfloat16
F32 = jnp.float32
LIVE, CENTRE, RATE, MEAN1, RATE1, COUNT, MEAN2, RATE2, LSE = range(9)


def grid_of(count):
    if count == 16:
        return (4, 2, 2)
    if count == 64:
        return (4, 4, 4)
    return (count, 1, 1)


class Grid:
    def __init__(self, dims):
        self.dims = dims
        self.index = lax.axis_index("dp")
        self.core = lax.axis_index("mp")
        _, second, third = dims
        self.place = (
            self.index // (second * third),
            lax.rem(self.index // third, second),
            lax.rem(self.index, third),
        )
        self.count = dims[0] * second * third

    def moved(self, axis, step):
        place = list(self.place)
        size = self.dims[axis]
        place[axis] = lax.rem(place[axis] + (step + size), size)
        return tuple(place)

    def device(self, place):
        _, second, third = self.dims
        return ((place[0] * second + place[1]) * third + place[2], self.core)

    def sibling(self):
        return (self.index, 1 - self.core)

    def beside(self, step, core):
        return (lax.rem(self.index + (step + self.count), self.count), core)

    def peers(self):
        out = [self.sibling()]
        for axis in range(3):
            for step in range(1, self.dims[axis]):
                out.append(self.device(self.moved(axis, step)))
        for step in (-1, 1):
            out += [self.beside(step, 0), self.beside(step, 1)]
        return out


def order_of(half):
    return (0, 1, 2) if half == 0 else (0, 2, 1)


def region(ref, half, stage, place, columns):
    at = list(place)
    for axis in order_of(half)[:stage]:
        at[axis] = slice(None)
    return ref.at[(at[0], at[1], at[2], slice(None), columns)]


def enter(peers):
    barrier = pltpu.get_barrier_semaphore()
    for peer in peers:
        pl.semaphore_signal(barrier, inc=1, device_id=peer, device_id_type=MESH)
    pl.semaphore_wait(barrier, len(peers))


def halves_of(start, size):
    if size % (2 * LANES):
        return ((start, size),)
    return ((start, size // 2), (start + size // 2, size // 2))


def remote(src, dst, send, recv, target):
    return pltpu.make_async_remote_copy(
        src_ref=src,
        dst_ref=dst,
        send_sem=send,
        recv_sem=recv,
        device_id=target,
        device_id_type=MESH,
    )


class Gather:
    def __init__(self, grid, ref, start, size, send, recv, slot, twin=None, pair=None):
        self.grid, self.ref, self.send, self.recv, self.slot = grid, ref, send, recv, slot
        self.parts = [pl.ds(s, n) for s, n in halves_of(start, size)]
        self.twin, self.pair = twin, pair

    def copy(self, half, stage, step, sender):
        axis = order_of(half)[stage]
        place = self.grid.place if sender else self.grid.moved(axis, -step)
        side = region(self.ref, half, stage, place, self.parts[half])
        sems = (self.slot, half, stage, step - 1)
        target = self.grid.device(self.grid.moved(axis, step))
        return remote(side, side, self.send.at[sems], self.recv.at[sems], target)

    def steps(self, stage):
        for half in range(len(self.parts)):
            for step in range(1, self.grid.dims[order_of(half)[stage]]):
                yield half, step

    def start(self, stage):
        for half, step in self.steps(stage):
            self.copy(half, stage, step, True).start()

    def arrive(self, stage):
        for half, step in self.steps(stage):
            self.copy(half, stage, step, False).wait_recv()

    def twin_copy(self, half, step):
        axis = order_of(half)[2]
        place = self.grid.place if step == 0 else self.grid.moved(axis, -step)
        src = region(self.ref, half, 2, place, self.parts[half])
        dst = region(self.twin, half, 2, place, self.parts[half])
        send, recv = self.pair
        sems = (self.slot, half, step)
        return remote(src, dst, send.at[sems], recv.at[sems], self.grid.sibling())

    def twin_steps(self):
        for half in range(len(self.parts)):
            for step in range(self.grid.dims[order_of(half)[2]]):
                yield half, step

    def tick(self, stage):
        self.arrive(stage)
        if stage < 2:
            self.start(stage + 1)
        if self.twin is not None and stage > 0:
            for half, step in self.twin_steps():
                if (step == 0) == (stage == 1):
                    self.twin_copy(half, step).start()

    def ready(self):
        if self.twin is not None:
            for half, step in self.twin_steps():
                self.twin_copy(half, step).wait_recv()

    def finish(self):
        for stage in range(3):
            for half, step in self.steps(stage):
                self.copy(half, stage, step, True).wait_send()
        if self.twin is not None:
            for half, step in self.twin_steps():
                self.twin_copy(half, step).wait_send()


class Scatter:
    def __init__(self, grid, ref, boxes, start, size, send, recv, slot, out):
        self.grid, self.ref, self.boxes, self.out = grid, ref, boxes, out
        self.send, self.recv, self.slot = send, recv, slot
        self.parts = [pl.ds(s, n) for s, n in halves_of(start, size)]

    def box(self, half, stage, step):
        full = (slice(None),) * (2 - stage)
        return self.boxes[stage].at[(step - 1, *full, slice(None), self.parts[half])]

    def copies(self, half, stage):
        axis = order_of(half)[2 - stage]
        out = []
        for step in range(1, self.grid.dims[axis]):
            place = self.grid.moved(axis, step)
            sems = (self.slot, half, stage, step - 1)
            src = region(self.ref, half, 2 - stage, place, self.parts[half])
            dst = self.box(half, stage, step)
            target = self.grid.device(place)
            out.append(remote(src, dst, self.send.at[sems], self.recv.at[sems], target))
        return out

    def start(self, stage):
        for half in range(len(self.parts)):
            for copy in self.copies(half, stage):
                copy.start()

    def tick(self, stage):
        for half in range(len(self.parts)):
            copies = self.copies(half, stage)
            for copy in copies:
                copy.wait_recv()
            mine = region(self.ref, half, 2 - stage, self.grid.place, self.parts[half])
            self.add(mine, half, stage, len(copies))
        if stage < 2:
            self.start(stage + 1)

    def add(self, mine, half, stage, count):
        lead = mine.shape[: 2 - stage]
        flat = 1
        for extent in lead:
            flat *= extent

        def one(item, _):
            at = ()
            if len(lead) == 2:
                at = (item // lead[1], lax.rem(item, lead[1]))
            elif len(lead) == 1:
                at = (item,)
            where = (*at, slice(None), slice(None))
            total = mine[where].astype(F32)
            for step in range(1, count + 1):
                total = total + self.box(half, stage, step)[where].astype(F32)
            if stage == 2:
                self.out[:, self.parts[half]] = total
            else:
                mine[where] = total.astype(mine.dtype)
            return 0

        if flat == 1:
            one(0, 0)
        else:
            lax.fori_loop(0, flat, one, 0)

    def finish(self):
        for half in range(len(self.parts)):
            for stage in range(3):
                for copy in self.copies(half, stage):
                    copy.wait_send()


def loop(count, body):
    def one(item, _):
        body(item)
        return 0

    lax.fori_loop(0, count, one, 0)


def at_rows(item, size):
    return pl.ds(pl.multiple_of(item * size, size), size)


def dot(left, right):
    return jnp.dot(left, right, preferred_element_type=F32)


def dot_t(left, right):
    return lax.dot_general(left, right, (((1,), (1,)), ((), ())), preferred_element_type=F32)


def t_dot(left, right):
    return lax.dot_general(left, right, (((0,), (0,)), ((), ())), preferred_element_type=F32)


def row_sum(value):
    return jnp.sum(value, axis=1, keepdims=True)


def series_sum(column):
    rows = column.shape[0]
    parts = column.reshape(rows // PAD, PAD, 1)
    total = jnp.sum(parts, axis=1, keepdims=True)
    return jnp.broadcast_to(total, parts.shape).reshape(rows, 1)


def split2(value):
    high = value.astype(BF16)
    return high, (value - high.astype(F32)).astype(BF16)


def fold8(value):
    return jnp.sum(value.reshape(value.shape[0] // 8, 8, value.shape[1]), axis=0)


def layer_kernel(dims, slots, *refs):
    (
        series, cotangent, block, small, live, offset,
        out_ref, grad_ref, sums, tiny_sums,
        w_own, w_twin, params_full, params, xp, cp, act1, qkv, mixed, hid, act2, slope, inner,
        ghid, stats, colsum, colsum_twin, g, stg, box0, box1, box2, sg, tbox0, tbox1, tbox2,
        y_tail, dx_tail,
        send, recv, pair_send, pair_recv, rs_send, rs_recv, stg_send, stg_recv, local, edge_send,
        edge_recv,
    ) = refs
    grid = Grid(dims)
    weights = (w_own, w_twin)
    rows, width = series.shape
    per = block.shape[0]
    mine = rows // 2
    pad_rows = mine // slots * PAD
    chunk = 256
    source = chunk // PAD * slots
    chunks = pad_rows // chunk
    blocks = pad_rows // LANES
    raw = mine + PAD
    heads = JOB // HDIM
    scale = HDIM ** (-0.5)
    quarter = width // dims[0]
    core = grid.core
    QC, KC, VC, OC, UC, DC = 0, JOB, 2 * JOB, 3 * JOB, 4 * JOB, 6 * JOB

    own = pltpu.make_async_copy(block, w_own.at[grid.place], local.at[0])
    own_small = pltpu.make_async_copy(small, params_full.at[grid.place], local.at[1])
    own.start()
    own_small.start()
    enter(grid.peers())
    own_small.wait()
    own.wait()
    njobs = block.shape[1] // JOB
    tiny_job = Gather(grid, params_full, 0, LANES, send, recv, njobs)
    jobs = [
        Gather(grid, w_own, j * JOB, JOB, send, recv, j, w_twin, (pair_send, pair_recv))
        for j in range(njobs)
    ]
    tiny_job.start(0)
    jobs[0].start(0)

    def edge_in(k, ref):
        return remote(
            ref.at[pl.ds(0, PAD)],
            inner.at[k, pl.ds(mine, PAD)],
            edge_send.at[k],
            edge_recv.at[k],
            grid.beside(-1, core),
        )

    pairs = ((0, series), (1, cotangent))
    first_row = pl.multiple_of(core * mine, PAD)

    def body_copy(k, ref):
        return pltpu.make_async_copy(
            ref.at[pl.ds(first_row, mine)], inner.at[k, pl.ds(0, mine)], local.at[2 + k]
        )

    def edge_copy(k, ref):
        return pltpu.make_async_copy(
            ref.at[pl.ds(mine, PAD)], inner.at[k, pl.ds(mine, PAD)], local.at[4 + k]
        )

    for k, ref in pairs:
        body_copy(k, ref).start()

    @pl.when(core == 1)
    def _():
        for k, ref in pairs:
            edge_in(k, ref).start()

    @pl.when(core == 0)
    def _():
        for k, ref in pairs:
            edge_copy(k, ref).start()
        for k, ref in pairs:
            edge_copy(k, ref).wait()

    for k, ref in pairs:
        body_copy(k, ref).wait()

    @pl.when(core == 1)
    def _():
        for k, ref in pairs:
            edge_in(k, ref).wait()

    shift = offset[0]

    def placing():
        row = lax.broadcasted_iota(jnp.int32, (chunk, chunk), 0)
        col = lax.broadcasted_iota(jnp.int32, (chunk, chunk), 1)
        slot = row & (PAD - 1)
        spot = slots * (row >> 4) + slot + shift
        return jnp.where((spot == col) & (slot < slots), 1.0, 0.0).astype(BF16)

    def pad_rows_of(k, target):
        place = placing()

        def body(item):
            part = inner[k, pl.ds(pl.multiple_of(item * source, PAD), chunk), :]
            target[at_rows(item, chunk), :] = dot(place, part).astype(BF16)

        loop(chunks, body)

    def fill_live():
        turned = live[...].T
        for b in range(blocks):
            stats[b * LANES : (b + 1) * LANES, :] = jnp.broadcast_to(
                turned[:, b : b + 1], (LANES, LANES)
            )

    lane_ids = lax.broadcasted_iota(jnp.int32, (LANES, LANES), 1)

    def stat(at, lane):
        return stats[at, lane : lane + 1]

    def first_stats():
        def body(b):
            at = at_rows(b, LANES)
            x = xp[at, :].astype(F32)
            alive = stat(at, LIVE)
            count = series_sum(alive) * width
            centre = series_sum(row_sum(x) * alive) / count
            centred = x - centre
            spread = series_sum(row_sum(centred * centred) * alive) / count
            rate = lax.rsqrt(spread + EPSILON)
            normed = centred * rate
            mean = row_sum(normed) * (1.0 / width)
            left = normed - mean
            rate1 = lax.rsqrt(row_sum(left * left) * (1.0 / width) + EPSILON)
            table = stats[at, :]
            for lane, value in (
                (CENTRE, centre), (RATE, rate), (MEAN1, mean), (RATE1, rate1), (COUNT, count),
            ):
                table = jnp.where(lane_ids == lane, value, table)
            stats[at, :] = table

        loop(blocks, body)

    def join_params():
        share = LANES // per
        _, second, third = dims
        for j in range(width // LANES):
            total = None
            for s in range(share):
                i = j * share + s
                part = params_full[i // (second * third), i // third % second, i % third]
                part = part.astype(F32)
                total = part if total is None else total + part
            params[:, j * LANES : (j + 1) * LANES] = total

    def normed_of(at):
        return (xp[at, :].astype(F32) - stat(at, CENTRE)) * stat(at, RATE)

    def first_act():
        gain, bias = params[0:1, :], params[1:2, :]

        def body(b):
            at = at_rows(b, LANES)
            left = (normed_of(at) - stat(at, MEAN1)) * stat(at, RATE1)
            act1[at, :] = (left * gain + bias).astype(BF16)

        loop(blocks, body)

    def whole_weight(h, start, size):
        return weights[h][:, :, :, :, pl.ds(start, size)].reshape(width, size)

    def some_rows(h, item, count, start, size):
        part = weights[h][pl.ds(item * count, count), :, :, :, pl.ds(start, size)]
        return part.reshape(count * quarter, size)

    def project(which):
        def body(m):
            at = at_rows(m, chunk)
            for h in range(2):
                made = dot(act1[at, :], whole_weight(h, which * JOB, JOB))
                qkv[h, at, which * JOB : (which + 1) * JOB] = made.astype(BF16)

        loop(chunks, body)

    def attention_bias(b):
        row = lax.broadcasted_iota(jnp.int32, (LANES, LANES), 0)
        col = lane_ids
        seen = live[pl.ds(b, 1), :] > 0.5
        allowed = ((row >> 4) == (col >> 4)) & (row >= col) & (seen | (row == col))
        return jnp.where(allowed, 0.0, MASKED)

    def head_at(which, hh):
        return pl.ds(which * JOB + hh * HDIM, HDIM)

    def attend(low, high):
        def body(item):
            b = low + item
            at = at_rows(b, LANES)
            bias = attention_bias(b)
            table = stats[at, :]
            for h in range(2):
                raw_s = [
                    dot_t(qkv[h, at, head_at(0, e)], qkv[h, at, head_at(1, e)])
                    for e in range(heads)
                ]
                raw_s = [s * scale + bias for s in raw_s]
                top = [jnp.max(s, axis=1, keepdims=True) for s in raw_s]
                expo = [jnp.exp(s - t) for s, t in zip(raw_s, top)]
                total = [row_sum(e) for e in expo]
                low_p = [(e / t).astype(BF16) for e, t in zip(expo, total)]
                for e in range(heads):
                    made = dot(low_p[e], qkv[h, at, head_at(2, e)])
                    mixed[h, at, e * HDIM : (e + 1) * HDIM] = made.astype(BF16)
                    table = jnp.where(
                        lane_ids == LSE + h * heads + e, top[e] + jnp.log(total[e]), table
                    )
            stats[at, :] = table

        loop(high - low, body)

    def out_project():
        def body(m):
            at = at_rows(m, chunk)
            for n in range(2):
                cols = slice(n * JOB, (n + 1) * JOB)
                made = (xp[at, cols].astype(F32) - stat(at, CENTRE)) * stat(at, RATE)
                for h in range(2):
                    made = made + dot_t(mixed[h, at, :], some_rows(h, n, dims[0] // 2, OC, JOB))
                hid[at, cols] = made

        loop(chunks, body)

    def second_act():
        gain, bias = params[2:3, :], params[3:4, :]

        def body(b):
            at = at_rows(b, LANES)
            value = hid[at, :]
            mean = row_sum(value) * (1.0 / width)
            left = value - mean
            rate = lax.rsqrt(row_sum(left * left) * (1.0 / width) + EPSILON)
            act2[at, :] = (left * rate * gain + bias).astype(BF16)
            table = jnp.where(lane_ids == MEAN2, mean, stats[at, :])
            stats[at, :] = jnp.where(lane_ids == RATE2, rate, table)

        loop(blocks, body)

    def feed(n):
        def body(m):
            at = at_rows(m, chunk)
            for h in range(2):
                gate = dot(act2[at, :], whole_weight(h, UC + n * JOB, JOB))
                share = 0.5 * (1.0 + lax.erf(gate * 0.7071067811865476))
                cols = slice(n * JOB, (n + 1) * JOB)
                inner[h, at, cols] = (gate * share).astype(BF16)
                made = share + gate * jnp.exp(-0.5 * gate * gate) * 0.3989422804014327
                if h == 0:
                    slope[0, at, cols], slope[1, at, cols] = split2(made)
                else:
                    ghid[at, cols] = made

        loop(chunks, body)

    boxes = (box0, box1, box2)
    scatters = {
        c: Scatter(grid, g, boxes, c * JOB, JOB, rs_send, rs_recv, c, sums) for c in range(njobs)
    }
    given = []

    def give_copy(c, slot):
        return remote(
            stg.at[slot],
            g.at[:, :, :, :, pl.ds(c * JOB, JOB)],
            stg_send.at[c],
            stg_recv.at[c],
            grid.sibling(),
        )

    def give(c, left, right):
        slot = len(given) % 2
        if len(given) >= 2:
            before, before_slot = given[-2]
            give_copy(before, before_slot).wait_send()
        given.append((c, slot))

        def body(a):
            made = t_dot(left[:, at_rows(a, quarter)], right(1)).astype(BF16)
            stg[slot, a] = made.reshape(dims[1], dims[2], per, JOB)

        loop(dims[0], body)
        give_copy(c, slot).start()

    def keep(c, left, right):
        slot = [s for k, s in given if k == c][0]
        give_copy(c, slot).wait_recv()
        cols = pl.ds(c * JOB, JOB)

        def body(a):
            made = t_dot(left[:, at_rows(a, quarter)], right(0))
            other = g[a, :, :, :, cols].reshape(quarter, JOB).astype(F32)
            g[a, :, :, :, cols] = (made + other).astype(BF16).reshape(
                dims[1], dims[2], per, JOB
            )

        loop(dims[0], body)
        scatters[c].start(0)

    def tick(*pairs):
        for c, stage in pairs:
            scatters[c].tick(stage)

    def inner_part(n):
        return lambda h: inner[h, :, n * JOB : (n + 1) * JOB]

    def slope_part(n):
        return lambda h: slope[h, :, n * JOB : (n + 1) * JOB]

    def mixed_part(h):
        return mixed[h]

    def qkv_part(which):
        return lambda h: qkv[h, :, which * JOB : (which + 1) * JOB]

    def grad_gate():
        def body(m):
            at = at_rows(m, chunk)
            for n in range(2):
                cols = slice(n * JOB, (n + 1) * JOB)
                made = [dot(cp[at, :], whole_weight(h, DC + n * JOB, JOB)) for h in range(2)]
                first = slope[0, at, cols].astype(F32) + slope[1, at, cols].astype(F32)
                slope[0, at, cols] = (made[0] * first).astype(BF16)
                slope[1, at, cols] = (made[1] * ghid[at, cols]).astype(BF16)

        loop(chunks, body)

    def back_project(target, parts, start, size):
        def body(m):
            at = at_rows(m, chunk)
            for n in range(2):
                made = None
                for h in range(2):
                    term = dot_t(parts[h, at, :], some_rows(h, n, dims[0] // 2, start, size))
                    made = term if made is None else made + term
                target[at, n * JOB : (n + 1) * JOB] = made

        loop(chunks, body)

    def norm_back(grad, hat, gain, rate):
        scaled = grad * gain
        mean = row_sum(scaled) * (1.0 / width)
        along = row_sum(scaled * hat) * (1.0 / width)
        return rate * (scaled - mean - hat * along)

    step_rows = LANES // 2

    def second_back():
        gain = params[2:3, :]

        def one(b, carry):
            at = at_rows(b, step_rows)
            grad = ghid[at, :]
            rate = stat(at, RATE2)
            hat = (hid[at, :] - stat(at, MEAN2)) * rate
            made = norm_back(grad, hat, gain, rate) + cp[at, :].astype(F32)
            ghid[at, :] = made
            act2[at, :] = made.astype(BF16)
            return carry[0] + fold8(grad * hat), carry[1] + fold8(grad)

        zero = jnp.zeros((8, width), F32)
        gains, biases = lax.fori_loop(0, pad_rows // step_rows, one, (zero, zero))
        colsum[2:3, :] = jnp.sum(gains, axis=0, keepdims=True)
        colsum[3:4, :] = jnp.sum(biases, axis=0, keepdims=True)

    def grad_mixed():
        def body(m):
            at = at_rows(m, chunk)
            for h in range(2):
                made = dot(act2[at, :], whole_weight(h, OC, JOB))
                cp[at, h * JOB : (h + 1) * JOB] = made.astype(BF16)

        loop(chunks, body)

    def attend_back(low, high):
        def body(item):
            b = low + item
            at = at_rows(b, LANES)
            bias = attention_bias(b)
            for h in range(2):
                every = range(heads)
                query = [qkv[h, at, head_at(0, e)] for e in every]
                keys = [qkv[h, at, head_at(1, e)] for e in every]
                values = [qkv[h, at, head_at(2, e)] for e in every]
                grads = [cp[at, h * JOB + e * HDIM : h * JOB + (e + 1) * HDIM] for e in every]
                raw_s = [dot_t(query[e], keys[e]) for e in every]
                grad_p = [dot_t(grads[e], values[e]) for e in every]
                lse = [stat(at, LSE + h * heads + e) for e in every]
                probs = [jnp.exp(raw_s[e] * scale + bias - lse[e]) for e in every]
                along = [row_sum(grad_p[e] * probs[e]) for e in every]
                grad_s = [(probs[e] * (grad_p[e] - along[e])).astype(BF16) for e in every]
                low_p = [p.astype(BF16) for p in probs]
                for e in every:
                    qkv[h, at, head_at(2, e)] = t_dot(low_p[e], grads[e]).astype(BF16)
                for e in every:
                    qkv[h, at, head_at(0, e)] = (dot(grad_s[e], keys[e]) * scale).astype(BF16)
                for e in every:
                    made = t_dot(grad_s[e], query[e]) * scale
                    qkv[h, at, head_at(1, e)] = made.astype(BF16)

        loop(high - low, body)

    def layer_out():
        def body(m):
            at = at_rows(m, chunk)
            for n in range(2):
                cols = slice(n * JOB, (n + 1) * JOB)
                made = hid[at, cols]
                for h in range(2):
                    made = made + dot_t(
                        inner[h, at, :], some_rows(h, n, dims[0] // 2, DC, 2 * JOB)
                    )
                act2[at, cols] = made.astype(BF16)

        loop(chunks, body)

    def first_back():
        gain = params[0:1, :]

        def one(b, carry):
            at = at_rows(b, step_rows)
            grad = hid[at, :]
            rate, rate1, count = stat(at, RATE), stat(at, RATE1), stat(at, COUNT)
            alive = stat(at, LIVE)
            centred = xp[at, :].astype(F32) - stat(at, CENTRE)
            hat = (centred * rate - stat(at, MEAN1)) * rate1
            made = norm_back(grad, hat, gain, rate1) + ghid[at, :]
            through = series_sum(row_sum(made * centred))
            spread_grad = -0.5 * rate * rate * rate * through
            pull = 2.0 * spread_grad / count
            centre_grad = -(
                rate * series_sum(row_sum(made)) + pull * series_sum(alive * row_sum(centred))
            )
            hid[at, :] = made * rate + alive * (pull * centred + centre_grad / count)
            return carry[0] + fold8(grad * hat), carry[1] + fold8(grad)

        zero = jnp.zeros((8, width), F32)
        gains, biases = lax.fori_loop(0, pad_rows // step_rows, one, (zero, zero))
        colsum[0:1, :] = jnp.sum(gains, axis=0, keepdims=True)
        colsum[1:2, :] = jnp.sum(biases, axis=0, keepdims=True)

    def unpad_rows(source_ref, tail_ref, target, exact):
        place = placing()
        row = lax.broadcasted_iota(jnp.int32, (PAD, PAD), 0)
        col = lax.broadcasted_iota(jnp.int32, (PAD, PAD), 1)
        late = jnp.where((row == col + (shift - slots)) & (col < slots), 1.0, 0.0).astype(BF16)

        def moved(matrix, value, first):
            if exact:
                return first(matrix, value)
            high, low = split2(value)
            return first(matrix, high) + first(matrix, low)

        for k in range(chunks):
            value = source_ref[k * chunk : (k + 1) * chunk, :]
            before = tail_ref[...] if k == 0 else source_ref[k * chunk - PAD : k * chunk, :]
            made = moved(place, value, t_dot)
            head = made[:PAD] + moved(late, before, dot)
            target[k * source : k * source + PAD, :] = head.astype(target.dtype)
            target[k * source + PAD : (k + 1) * source, :] = made[PAD:source].astype(target.dtype)

    ahead = grid.beside(core, 1 - core)

    def tail_copy(k, ref, target):
        return remote(
            ref.at[pl.ds(pad_rows - PAD, PAD)], target, edge_send.at[k], edge_recv.at[k], ahead
        )

    tiny_scatter = Scatter(
        grid, sg, (tbox0, tbox1, tbox2), 0, LANES, rs_send, rs_recv, njobs, tiny_sums
    )
    colsum_copy = remote(
        colsum, colsum_twin, edge_send.at[4], edge_recv.at[4], grid.sibling()
    )

    def spread_tiny():
        share = LANES // per
        _, second, third = dims
        for i in range(grid.count):
            j = i // share
            cols = slice(j * LANES, (j + 1) * LANES)
            sg[i // (second * third), i // third % second, i % third] = (
                colsum[:, cols] + colsum_twin[:, cols]
            )

    def grad_copy(where):
        at = pl.ds(first_row, mine)
        if where == "here":
            return pltpu.make_async_copy(ghid.at[pl.ds(0, mine)], grad_ref.at[at], local.at[2])
        return remote(
            ghid.at[pl.ds(0, mine)],
            grad_ref.at[at],
            edge_send.at[5],
            edge_recv.at[5],
            grid.sibling(),
        )

    out_copy = pltpu.make_async_copy(cp.at[pl.ds(0, mine)], out_ref, local.at[3])

    def gather_tick(t):
        if t < njobs:
            jobs[t].tick(0)
            if t + 1 < njobs:
                jobs[t + 1].start(0)
        if 0 <= t - 1 < njobs:
            jobs[t - 1].tick(1)
        if 0 <= t - 2 < njobs:
            jobs[t - 2].tick(2)

    pad_rows_of(0, xp)
    gather_tick(0)
    tiny_job.tick(0)
    fill_live()
    first_stats()
    pad_rows_of(1, cp)
    gather_tick(1)
    tiny_job.tick(1)
    gather_tick(2)
    tiny_job.tick(2)
    colsum[...] = jnp.zeros_like(colsum)
    join_params()
    first_act()
    jobs[0].ready()
    project(0)
    gather_tick(3)
    jobs[1].ready()
    project(1)
    gather_tick(4)
    jobs[2].ready()
    project(2)
    gather_tick(5)
    attend(0, blocks // 2)
    gather_tick(6)
    attend(blocks // 2, blocks)
    jobs[3].ready()
    out_project()
    gather_tick(7)
    second_act()
    jobs[4].ready()
    feed(0)
    gather_tick(8)
    jobs[5].ready()
    feed(1)
    gather_tick(9)

    cq, ck, cv, co, cu, cd = (QC // JOB, KC // JOB, VC // JOB, OC // JOB, UC // JOB, DC // JOB)
    give(cd, cp, inner_part(0))
    give(cd + 1, cp, inner_part(1))
    keep(cd, cp, inner_part(0))
    keep(cd + 1, cp, inner_part(1))
    jobs[6].ready()
    jobs[7].ready()
    grad_gate()
    give(cu, act2, slope_part(0))
    tick((cd, 0))
    give(cu + 1, act2, slope_part(1))
    tick((cd + 1, 0))
    keep(cu, act2, slope_part(0))
    keep(cu + 1, act2, slope_part(1))
    tick((cd, 1), (cd + 1, 1))
    back_project(ghid, slope, UC, 2 * JOB)
    tick((cu, 0), (cd, 2), (cu + 1, 0), (cd + 1, 2))
    second_back()
    tick((cu, 1), (cu + 1, 1))
    give(co, act2, mixed_part)
    grad_mixed()
    keep(co, act2, mixed_part)
    attend_back(0, blocks // 3)
    tick((cu, 2), (cu + 1, 2), (co, 0))
    attend_back(blocks // 3, 2 * blocks // 3)
    tick((co, 1))
    attend_back(2 * blocks // 3, blocks)
    tick((co, 2))
    give(cq, act1, qkv_part(0))
    give(ck, act1, qkv_part(1))
    keep(cq, act1, qkv_part(0))
    give(cv, act1, qkv_part(2))
    keep(ck, act1, qkv_part(1))
    keep(cv, act1, qkv_part(2))
    layer_out()
    tail_copy(2, act2, y_tail).start()
    tick((cq, 0), (ck, 0))
    back_project(hid, qkv, 0, 3 * JOB)
    tick((cv, 0), (cq, 1))
    first_back()
    tail_copy(3, hid, dx_tail).start()
    colsum_copy.start()
    tick((ck, 1), (cv, 1))
    tail_copy(2, act2, y_tail).wait_recv()
    unpad_rows(act2, y_tail, cp, True)
    out_copy.start()
    colsum_copy.wait_recv()
    spread_tiny()
    tiny_scatter.start(0)
    tail_copy(3, hid, dx_tail).wait_recv()
    unpad_rows(hid, dx_tail, ghid, False)
    grad_copy("here").start()
    grad_copy("there").start()
    tiny_scatter.tick(0)
    tick((cq, 2))
    tiny_scatter.tick(1)
    tick((ck, 2))
    tiny_scatter.tick(2)
    tick((cv, 2))

    for job in [tiny_job, *jobs]:
        job.finish()
    for job in [tiny_scatter, *scatters.values()]:
        job.finish()
    for c, slot in given[-2:]:
        give_copy(c, slot).wait_send()
    tail_copy(2, act2, y_tail).wait_send()
    tail_copy(3, hid, dx_tail).wait_send()
    colsum_copy.wait_send()
    out_copy.wait()
    grad_copy("here").wait()
    grad_copy("there").wait()


def box_shapes(dims, shape, dtype):
    most = max(max(dims[1:]) - 1, 1)
    return [
        pltpu.VMEM((most, dims[0], dims[1], *shape), dtype),
        pltpu.VMEM((most, dims[0], *shape), dtype),
        pltpu.VMEM((max(dims[0] - 1, 1), *shape), dtype),
    ]


def layer(series, cotangent, block, small, live, offset, dims, slots):
    rows, width = series.shape
    per, columns = block.shape
    mine = rows // 2
    pad = mine // slots * PAD
    most = max(dims) - 1
    njobs = columns // JOB
    anywhere = pl.BlockSpec(memory_space=pl.ANY)
    vmem = pl.BlockSpec(memory_space=pltpu.VMEM)
    dma = pltpu.SemaphoreType.DMA
    return pl.pallas_call(
        functools.partial(layer_kernel, dims, slots),
        out_shape=(
            jax.ShapeDtypeStruct((mine, width), BF16),
            jax.ShapeDtypeStruct((rows, width), F32),
            jax.ShapeDtypeStruct((per, columns), F32),
            jax.ShapeDtypeStruct((8, LANES), F32),
        ),
        in_specs=[
            anywhere, anywhere, anywhere, anywhere, vmem,
            pl.BlockSpec(memory_space=pltpu.SMEM),
        ],
        out_specs=(anywhere, anywhere, vmem, vmem),
        scratch_shapes=[
            pltpu.VMEM((*dims, per, columns), BF16),
            pltpu.VMEM((*dims, per, columns), BF16),
            pltpu.VMEM((*dims, PAD, LANES), BF16),
            pltpu.VMEM((PAD, width), F32),
            pltpu.VMEM((pad, width), BF16),
            pltpu.VMEM((pad, width), BF16),
            pltpu.VMEM((pad, width), BF16),
            pltpu.VMEM((2, pad, 3 * JOB), BF16),
            pltpu.VMEM((2, pad, JOB), BF16),
            pltpu.VMEM((pad, width), F32),
            pltpu.VMEM((pad, width), BF16),
            pltpu.VMEM((2, pad, 2 * JOB), BF16),
            pltpu.VMEM((2, pad, 2 * JOB), BF16),
            pltpu.VMEM((pad, width), F32),
            pltpu.VMEM((pad, LANES), F32),
            pltpu.VMEM((8, width), F32),
            pltpu.VMEM((8, width), F32),
            pltpu.VMEM((*dims, per, columns), BF16),
            pltpu.VMEM((2, *dims, per, JOB), BF16),
            *box_shapes(dims, (per, columns), BF16),
            pltpu.VMEM((*dims, 8, LANES), F32),
            *box_shapes(dims, (8, LANES), F32),
            pltpu.VMEM((PAD, width), BF16),
            pltpu.VMEM((PAD, width), F32),
            dma((njobs + 1, 2, 3, most)),
            dma((njobs + 1, 2, 3, most)),
            dma((njobs, 2, most + 1)),
            dma((njobs, 2, most + 1)),
            dma((njobs + 1, 2, 3, most)),
            dma((njobs + 1, 2, 3, most)),
            dma((njobs,)),
            dma((njobs,)),
            dma((6,)),
            dma((6,)),
            dma((6,)),
        ],
        compiler_params=pltpu.CompilerParams(
            collective_id=0, has_side_effects=True, vmem_limit_bytes=VMEM_LIMIT
        ),
        name="decoder_layer",
    )(series, cotangent, block, small, live, offset)


VMEM_LIMIT = 64 << 20


def spread_params(stacked):
    per = stacked.shape[1]
    share = LANES // per
    spot = lax.rem(lax.axis_index("dp"), share)
    parts = [jnp.where(spot == s, stacked, jnp.zeros_like(stacked)) for s in range(share)]
    wide = jnp.concatenate(parts, axis=1)
    return jnp.pad(wide, ((0, PAD - stacked.shape[0]), (0, 0)))


def per_device(
    series_input,
    lookback,
    slot_mask,
    offset,
    query_weight,
    key_weight,
    value_weight,
    out_weight,
    up_weight,
    down_weight,
    first_gain,
    first_bias,
    second_gain,
    second_bias,
    cotangent,
):
    slots = slot_mask.shape[1]
    dims = grid_of(lax.axis_size("dp"))
    per = first_gain.shape[0]
    share = LANES // per
    count = slot_mask.shape[0] // 2
    first = lax.axis_index("mp") * count
    mask = lax.dynamic_slice_in_dim(slot_mask, first, count)
    back = lax.dynamic_slice_in_dim(lookback, first, count)
    slot_ids = lax.broadcasted_iota(jnp.int32, mask.shape, 1)
    live = (slot_ids >= slots - back[:, None]) & ((mask > 0) | (slot_ids == slots - 1))
    live = jnp.pad(live.astype(F32), ((0, 0), (0, PAD - slots))).reshape(-1, LANES)
    live = jnp.pad(live, ((0, -live.shape[0] % 8), (0, 0)))
    block = jnp.concatenate(
        [query_weight, key_weight, value_weight, out_weight.T, up_weight, down_weight.T], axis=1
    )
    small = spread_params(jnp.stack([first_gain, first_bias, second_gain, second_bias]))
    result, grad_input, sums, tiny = layer(
        series_input, cotangent, block, small, live, offset.reshape(1), dims, slots
    )
    spot = lax.rem(lax.axis_index("dp"), share)
    own = lax.dynamic_slice_in_dim(tiny, spot * per, per, axis=1)
    return (
        result,
        grad_input,
        sums[:, 0:512],
        sums[:, 512:1024],
        sums[:, 1024:1536],
        sums[:, 1536:2048].T,
        sums[:, 2048:3072],
        sums[:, 3072:4096].T,
        own[0],
        own[1],
        own[2],
        own[3],
    )


def solution(mesh):
    return jax.shard_map(
        per_device,
        mesh=mesh,
        in_specs=(
            P("dp", None),
            P("dp"),
            P("dp", None),
            P(),
            P("dp", "mp"),
            P("dp", "mp"),
            P("dp", "mp"),
            P("mp", "dp"),
            P("dp", "mp"),
            P("mp", "dp"),
            P("dp"),
            P("dp"),
            P("dp"),
            P("dp"),
            P("dp", None),
        ),
        out_specs=(
            P(("dp", "mp"), None),
            P("dp", None),
            P("dp", "mp"),
            P("dp", "mp"),
            P("dp", "mp"),
            P("mp", "dp"),
            P("dp", "mp"),
            P("mp", "dp"),
            P("dp"),
            P("dp"),
            P("dp"),
            P("dp"),
        ),
        check_vma=False,
    )
```

time: 1120 us -> 237 us (0.21)
  waiting for transfers between devices: 672 us -> 0 us
  Pallas kernels: 0 us -> 210 us
  matrix products: 137 us -> 0 us
  blocking collectives: 121 us -> 0 us
  other arithmetic: 71.6 us -> 3.5 us
  local copies, waits for them, and re-layouts: 83.4 us -> 21.8 us
  between operations: 17.4 us -> 1.33 us
  starting transfers between devices: 12 us -> 0 us
    reduce_scatter x6 -> x0, waiting for transfers between devices: 400 us -> none  [the longest x1 82.8 us: per_device(): lax.psum_scatter(out_delta, 'dp', scatter_dimension=1, tiled=True)]
    all_gather x6 -> x0, waiting for transfers between devices: 215 us -> none  [the longest x1 54.4 us: per_device(): lax.all_gather(up_weight, 'dp', axis=0, tiled=True)]
    pallas_call x0 -> x1, Pallas kernels: none -> 210 us  [layer(): pl.pallas_call(functools.partial(layer_kernel, dims, slots), out_shape=(j...]
    dot_general x38 -> x0, matrix products: 137 us -> none  [the longest x1 10.1 us: per_device(): jnp.einsum('tf,td->fd', inner, grad_ffn, preferred_element_type=jnp.float32)]
    unnamed x2 -> x0, blocking collectives: 121 us -> none
    psum x3 -> x0, waiting for transfers between devices: 50 us -> none  [the longest x1 28.9 us: per_device(): hidden_one = normed_own + lax.psum(attn_part, 'mp')]
    reduce_sum x14 -> x0, other arithmetic: 40 us -> none  [the longest x2 12.3 us: layer_norm(): return centred * lax.rsqrt(spread + EPSILON) * gain + shift]
    concatenate x4 -> x1, local copies, waits for them, and re-layouts: 31.4 us -> 1.57 us  [per_device(): jnp.concatenate([query_weight, key_weight, value_weight, out_weight.T, up...]
  transfers between devices with their start and end apart: 21 -> 0, of which waited for: 13 -> 0; matrix products, arithmetic and copies ran while one was open for 17% -> 0% of each run, Pallas kernels for 0% -> 0%
where the time goes in v1:
time: 237 us; the launch traced here: 236 us
  Pallas kernels  210 us (89%)
  local copies, waits for them, and re-layouts  21.8 us (9%)
  other arithmetic  3.5 us (1%)
    pallas_call x1, Pallas kernels, layer(): pl.pallas_call(functools.partial(layer_kernel, dims, slots), out_shape=(j...  210 us
    unnamed x10, local copies, waits for them, and re-layouts  14.9 us

profile of v1, /device:TPU:0, one launch (start us, length us, event | category | flops | bytes accessed | tf_op | source)
XLA Modules:
  0.0 236.4 jit_solution(380215545111165283)
XLA Ops:
  1.3 0.7 dynamic-slice_subtract_fusion
  2.0 0.8 fusion.2
  2.8 0.7 broadcast_select_fusion.1
  3.5 0.7 fusion.4.refs_3_
  4.2 0.1 copy.29
  4.3 0.1 reshape.33
  4.4 0.6 pad_convert_fusion.refs_4_
  5.0 1.5 constant_dynamic-update-slice_fusion.3
  6.5 1.5 constant_dynamic-update-slice_fusion.2
  8.0 1.5 constant_dynamic-update-slice_fusion.1
  9.4 1.5 bitcast_dynamic-update-slice_fusion.1
  10.9 1.6 constant_dynamic-update-slice_fusion
  12.5 1.6 bitcast_dynamic-update-slice_fusion.refs_2_
  14.0 209.8 %decoder_layer.1 = (bf16[720,1024]{1,0:T(8,128)(2,1)}, f32[1440,1024]{1,0:T(8,128)}, f32[64,4096]{1,0:T(8,128)}, f32[8,128]{1,0:T(8,128)}) custom-call(bf16[1440,1024]{1,0:T(8,128)(2,1)} %refs_0_.1, bf16[1440,1024]{1,0:T(8,128)(2,1)} %refs_1_.1, bf16[64,4096]{1,0:T(8,128)(2,1)} %bitcast_dynamic-update-slice_fusion.refs_2_, bf16[16,128]{1,0:T(8,128)(2,1)} %fusion.4.refs_3_, ...), custom_call_target="tpu_custom_call" | custom-call | tf_op jit(solution)/shard_map/decoder_layer/pallas_call | solution.py:927
  223.8 0.0 copy-start
  223.8 0.9 constant_dynamic-slice_fusion
  224.7 0.5 slice_bitcast_fusion.2
  225.2 1.9 slice_bitcast_fusion.1
  227.1 1.9 slice_bitcast_fusion
  229.0 0.0 copy-done
  229.0 1.1 copy.38
  230.1 6.3 %copy.39 = f32[1440,1024]{1,0:T(8,128)} copy(f32[1440,1024]{1,0:T(8,128)} %get-tuple-element.45) | data formatting | bytes 11796480
  (2 shorter events, 0.0 us)
Async XLA Ops:
  223.8 5.2 %copy-start = (bf16[720,1024]{1,0:T(8,128)(2,1)S(1)}, bf16[720,1024]{1,0:T(8,128)(2,1)}, u32[]{:S(2)}) copy-start(bf16[720,1024]{1,0:T(8,128)(2,1)} %get-tuple-element.44) | copy-start | bytes 4423684
